TPU v7x, 256 devices: a whole 4x4x8 slice. The times are simulated.
256 devices in a mesh: view: 8 (over y, core), tm: 16 (over z_lo, x), height: 2 (over z_hi).
Axes of the slice: x: 4, y: 4, z: 8 (z_hi: 2, z_lo: 4; z = z_hi * 4 + z_lo), core: 2. Of those that a mesh axis runs over, the one named last changes fastest.
Arguments:
- query_vectors: bfloat16 [8, 16, 8, 64, 1536], P('view', 'tm', 'height'), may hold values from -120 to 120
- key_vectors: bfloat16 [8, 16, 8, 64, 1536], P('view', 'tm', 'height'), may hold values from -6 to 6
- value_vectors: bfloat16 [8, 16, 8, 64, 1536], P('view', 'tm', 'height'), may hold values from -6 to 6
- out_grad: bfloat16 [8, 16, 8, 64, 1536], P('view', 'tm', 'height'), may hold values from -6 to 6
- epi_rows: int32 [8, 16, 2, 7], P(None, 'tm'), may hold values from 0 to 7
Outputs:
- attended: bfloat16 [8, 16, 8, 64, 1536], P('view', 'tm', 'height')
- query_grad: bfloat16 [8, 16, 8, 64, 1536], P('view', 'tm', 'height')
- key_grad: bfloat16 [8, 16, 8, 64, 1536], P('view', 'tm', 'height')
- value_grad: bfloat16 [8, 16, 8, 64, 1536], P('view', 'tm', 'height')
Inputs may be any that keep to these rules, and one draw needn't show every extreme that they name: epi_rows[v, f, b, d - 1] is the row of view (v + d) mod 8 in frame f that holds the epipolar line of query tile b of view v and frame f.
All inputs are finite; a program needn't handle non-finite values.
Results may differ from a plain program's by a relative error of at most 0.0056.
Values may be sent and summed in bfloat16 or wider, within the bound.
A program may use at most 128 MiB of HBM per device.

v0:
```python
import jax
import jax.numpy as jnp
from jax import lax
from jax.sharding import PartitionSpec as P

HEAD_DIM = 128


def from_behind(value, axis, by):
    devices = lax.axis_size(axis)
    pairs = [(i, i + by) for i in range(devices) if 0 <= i + by < devices]
    return lax.ppermute(value, axis, pairs)


def head_pass(query_rows, key_rows, value_rows, grad_rows, usable, score_scale):
    scores = (
        jnp.einsum("ne,me->nm", query_rows, key_rows, preferred_element_type=jnp.float32)
        * score_scale
    )
    scores = jnp.where(usable[None, :], scores, -1e30)
    row_max = jnp.max(scores, axis=1, keepdims=True)
    weights = jnp.exp(scores - row_max)
    normalized = weights / jnp.sum(weights, axis=1, keepdims=True)
    normalized_low = normalized.astype(jnp.bfloat16)
    attended = jnp.einsum(
        "nm,me->ne", normalized_low, value_rows, preferred_element_type=jnp.float32
    ).astype(jnp.bfloat16)
    grad_weights = jnp.einsum(
        "ne,me->nm", grad_rows, value_rows, preferred_element_type=jnp.float32
    )
    row_delta = jnp.sum(
        grad_rows.astype(jnp.float32) * attended.astype(jnp.float32), axis=1, keepdims=True
    )
    score_grad = (normalized * (grad_weights - row_delta)).astype(jnp.bfloat16)
    query_grad = (
        jnp.einsum("nm,me->ne", score_grad, key_rows, preferred_element_type=jnp.float32)
        * score_scale
    ).astype(jnp.bfloat16)
    key_terms = (
        jnp.einsum("nm,ne->me", score_grad, query_rows, preferred_element_type=jnp.float32)
        * score_scale
    )
    value_terms = jnp.einsum(
        "nm,ne->me", normalized_low, grad_rows, preferred_element_type=jnp.float32
    )
    return (attended, query_grad, key_terms, value_terms)


def body(query_vectors, key_vectors, value_vectors, out_grad, epi_rows):
    view_count = lax.axis_size("view")
    band_count = lax.axis_size("height")
    view_index = lax.axis_index("view")
    band_index = lax.axis_index("height")
    frame_index = lax.axis_index("tm")
    tile_rows = query_vectors.shape[2]
    columns = query_vectors.shape[3]
    features = query_vectors.shape[4]
    head_count = features // HEAD_DIM
    tokens = tile_rows * columns
    group_size = view_count * band_count
    score_scale = HEAD_DIM ** (-0.5)
    pair_rows = jnp.stack((key_vectors[0, 0], value_vectors[0, 0]))
    earlier_pair = from_behind(pair_rows, "tm", 1)
    request_table = epi_rows[:, 0]
    viewers = jnp.arange(view_count, dtype=jnp.int32)
    heights = jnp.arange(band_count, dtype=jnp.int32)
    offsets = jnp.arange(view_count - 1, dtype=jnp.int32)
    their_offset = (view_index - viewers) % view_count
    their_pick = (offsets[None, :] == their_offset[:, None] - 1).astype(jnp.int32)
    their_rows = jnp.sum(request_table * their_pick[:, None, :], axis=2)
    local_rows = band_index * tile_rows + jnp.arange(tile_rows, dtype=jnp.int32)
    chosen = (their_rows[:, :, None] == local_rows[None, None, :]) & (their_offset != 0)[
        :, None, None
    ]
    selector = chosen.reshape(group_size, tile_rows).astype(jnp.bfloat16)
    outgoing = jnp.einsum("jr,srcf->jscf", selector, pair_rows, preferred_element_type=jnp.bfloat16)
    incoming = lax.all_to_all(outgoing, ("view", "height"), split_axis=0, concat_axis=0, tiled=True)
    remote = incoming.reshape(view_count, band_count, 2, columns, features).sum(axis=1)
    key_set = jnp.concatenate(
        [
            pair_rows[0].reshape(tokens, features),
            earlier_pair[0].reshape(tokens, features),
            remote[:, 0].reshape(view_count * columns, features),
        ],
        axis=0,
    )
    value_set = jnp.concatenate(
        [
            pair_rows[1].reshape(tokens, features),
            earlier_pair[1].reshape(tokens, features),
            remote[:, 1].reshape(view_count * columns, features),
        ],
        axis=0,
    )
    usable = jnp.concatenate(
        [
            jnp.ones((tokens,), bool),
            jnp.broadcast_to(frame_index > 0, (tokens,)),
            jnp.repeat(viewers != view_index, columns),
        ]
    )

    def heads_first(array):
        return jnp.moveaxis(array.reshape(array.shape[0], head_count, HEAD_DIM), 1, 0)

    def tokens_first(array):
        return jnp.moveaxis(array, 0, 1).reshape(array.shape[1], features)

    def one_head(parts):
        return head_pass(parts[0], parts[1], parts[2], parts[3], usable, score_scale)

    head_inputs = (
        heads_first(query_vectors.reshape(tokens, features)),
        heads_first(key_set),
        heads_first(value_set),
        heads_first(out_grad.reshape(tokens, features)),
    )
    attended, query_grad, key_terms, value_terms = lax.map(one_head, head_inputs)
    attended = tokens_first(attended)
    query_grad = tokens_first(query_grad)
    key_terms = tokens_first(key_terms)
    value_terms = tokens_first(value_terms)
    earlier_terms = jnp.stack(
        (key_terms[tokens : 2 * tokens], value_terms[tokens : 2 * tokens])
    ).astype(jnp.bfloat16)
    later_terms = from_behind(earlier_terms, "tm", -1)
    far_terms = jnp.stack(
        (
            key_terms[2 * tokens :].reshape(view_count, columns, features),
            value_terms[2 * tokens :].reshape(view_count, columns, features),
        ),
        axis=1,
    ).astype(jnp.bfloat16)
    my_offset = (viewers - view_index) % view_count
    my_mask = (
        (viewers == view_index)[:, None, None] & (heights == band_index)[None, :, None]
    ).astype(jnp.int32)
    my_table = jnp.sum(request_table * my_mask, axis=(0, 1))
    my_rows = jnp.sum(
        my_table[None, :] * (offsets[None, :] == my_offset[:, None] - 1).astype(jnp.int32), axis=1
    )
    return_route = (my_rows[:, None] // tile_rows == heights[None, :]) & (my_offset != 0)[:, None]
    returning = far_terms[:, None] * return_route[:, :, None, None, None].astype(jnp.bfloat16)
    arrived = lax.all_to_all(
        returning.reshape(group_size, 2, columns, features),
        ("view", "height"),
        split_axis=0,
        concat_axis=0,
        tiled=True,
    )
    gathered_terms = jnp.einsum(
        "jr,jscf->srcf", selector, arrived, preferred_element_type=jnp.float32
    )
    own_terms = jnp.stack((key_terms[:tokens], value_terms[:tokens])).reshape(
        2, tile_rows, columns, features
    )
    summed_terms = (
        own_terms
        + later_terms.reshape(2, tile_rows, columns, features).astype(jnp.float32)
        + gathered_terms
    )
    out_shape = query_vectors.shape
    key_grad = summed_terms[0].astype(jnp.bfloat16).reshape(out_shape)
    value_grad = summed_terms[1].astype(jnp.bfloat16).reshape(out_shape)
    return (attended.reshape(out_shape), query_grad.reshape(out_shape), key_grad, value_grad)


def solution(mesh):
    placed = (
        P("view", "tm", "height", None, None),
        P("view", "tm", "height", None, None),
        P("view", "tm", "height", None, None),
        P("view", "tm", "height", None, None),
        P(None, "tm", None, None),
    )
    return jax.shard_map(
        body,
        mesh=mesh,
        in_specs=placed,
        out_specs=(
            P("view", "tm", "height", None, None),
            P("view", "tm", "height", None, None),
            P("view", "tm", "height", None, None),
            P("view", "tm", "height", None, None),
        ),
        check_vma=False,
    )
```

profile of v0, /device:TPU:22, one launch (start us, length us, event | category | flops | bytes accessed | tf_op | source)
XLA Modules:
  0.0 592.7 jit_solution(14196246085680053971)
XLA Ops:
  2.0 2.6 copy_bitcast_fusion
  4.6 2.6 fusion.49
  7.3 6.1 %copy.75 = bf16[16,2,64,1536]{3,2,1,0:T(8,128)(2,1)} copy(bf16[16,2,64,1536]{3,0,2,1:T(8,128)(2,1)S(1)} %fusion.49) | data formatting | bytes 12582912 | tf_op jit(solution)/shard_map/jr,srcf->jscf/dot_general | solution.py:76
  13.3 11.5 %all-to-all-start = ((bf16[16,2,64,1536]{3,2,1,0:T(8,128)(2,1)}), bf16[16,2,64,1536]{3,2,1,0:T(8,128)(2,1)}, u32[]{:S(2)}, u32[]{:S(2)}) async-start(bf16[16,2,64,1536]{3,2,1,0:T(8,128)(2,1)} %copy.75), calls=%async_computation | async-start | bytes 12582912 | tf_op jit(solution)/shard_map/all_to_all | solution.py:77
  24.8 2.4 pad_maximum_fusion.1
  27.2 3.4 collective-permute-start
  32.3 2.4 concatenate.34
  40.0 154.8 %collective-permute-done = bf16[2,4,64,1536]{3,1,2,0:T(4,128)(2,1)} collective-permute-done((bf16[2,4,64,1536]{3,1,2,0:T(4,128)(2,1)}, bf16[2,4,64,1536]{3,1,2,0:T(4,128)(2,1)}, u32[]{:S(2)}, u32[]{:S(2)}) %collective-permute-start) | collective-permute-done | bytes 1572896 | tf_op jit(solution)/shard_map/ppermute | solution.py:12
  194.8 1.9 fusion.64
  200.0 4.0 bitcast_reduce_fusion
  204.0 1.9 slice_bitcast_fusion
  206.0 2.9 concatenate.36
  208.9 2.4 maximum_bitcast_fusion.1
  211.3 2.4 copy.83
  213.7 2.9 concatenate.32
  216.6 2.2 maximum_bitcast_fusion
  218.9 2.4 copy.82
  221.3 138.5 %while.16 = (s32[]{:T(128)}, bf16[12,256,128]{1,2,0:T(8,128)(2,1)S(1)}, bf16[12,256,128]{2,1,0:T(8,128)(2,1)}, f32[12,1024,128]{1,2,0:T(8,128)}, f32[12,1024,128...) while((s32[]{:T(128)}, ...), condition=%wide.region_6.7_spmd, body=%wide.region_2.6_spmd.sunk | while | flops 407207168 | bytes 11617409 | solution.py:118
  230.1 2.1 fusion.95
  241.7 2.1 fusion.95
  253.2 2.0 fusion.95
  264.7 2.1 fusion.95
  276.2 2.1 fusion.95
  287.8 2.1 fusion.95
  299.4 2.0 fusion.95
  310.9 2.0 fusion.95
  322.4 2.1 fusion.95
  332.0 1.9 fusion.93
  333.9 2.1 fusion.95
  345.4 2.0 fusion.95
  357.0 2.0 fusion.95
  360.7 3.3 bitcast_convert_fusion
  365.4 4.4 copy.96
  369.8 4.0 stack.39
  373.7 3.3 bitcast_convert_fusion.1
  380.1 4.4 copy.95
  384.5 4.0 stack.38
  388.4 6.6 %bitcast_multiply_fusion = bf16[16,2,64,1536]{3,2,1,0:T(8,128)(2,1)} fusion(bf16[16]{0:T(256)(128)(2,1)S(1)} %reshape.297, bf16[8,1,64,1536]{3,2,0,1:T(8,128)(2,1)} %stack.39, bf16[8,1,64,1536]{3,2,0,1:T(8,128)(2,1)} %stack.38), kind=kLoop, calls=%fused_computation.44 | loop fusion | flops 14155776 | bytes 9437216 | tf_op jit(solution)/shard_map/mul | solution.py:143
  395.0 8.9 %all-to-all-start.1 = ((bf16[16,2,64,1536]{3,2,1,0:T(8,128)(2,1)}), bf16[16,2,64,1536]{3,2,1,0:T(8,128)(2,1)}, u32[]{:S(2)}, u32[]{:S(2)}) async-start(bf16[16,2,64,1536]{3,2,1,0:T(8,128)(2,1)} %bitcast_multiply_fusion), calls=%async_computation.1 | async-start | bytes 12582912 | tf_op jit(solution)/shard_map/all_to_all | solution.py:144
  406.4 1.9 collective-permute-start.1
  412.9 2.7 slice.64
  415.6 2.8 reshape.299
  418.5 2.5 copy.91
  421.0 2.7 slice.65
  423.7 2.8 reshape.300
  426.5 2.6 copy.92
  429.1 149.6 %collective-permute-done.1 = bf16[2,256,1536]{1,2,0:T(8,128)(2,1)} collective-permute-done((bf16[2,256,1536]{1,2,0:T(8,128)(2,1)}, bf16[2,256,1536]{1,2,0:T(8,128)(2,1)}, u32[]{:S(2)}, u32[]{:S(2)}) %collective-permute-start.1) | collective-permute-done | bytes 1572896 | tf_op jit(solution)/shard_map/ppermute | solution.py:12
  580.4 9.4 %fusion.42 = bf16[2,4,64,1536]{3,1,2,0:T(4,128)(2,1)S(1)} fusion(f32[1,4,64,1536]{3,1,2,0:T(4,128)} %copy.92, f32[1,4,64,1536]{3,1,2,0:T(4,128)} %copy.91, f32[2,4,64,1536]{3,2,1,0:T(8,128)S(1)} %bitcast.152, bf16[16,2,64,1536]{3,2,1,0:T(8,128)(2,1)} %all-to-all-done.1, s32[16]{0:T(128)S(1)} %eq.88, pred[16]{0:T(512)(128)(4,1)S(1)} %and.100, ...), kind=kOutput, calls=%fused_computation.53 | convolution fusion | flops 28311680 | bytes 14155872 | tf_op jit(solution)/shard_map/jr,jscf->srcf/dot_general | solution.py:151
  (169 shorter events, 139.6 us)
Async XLA Ops:
  13.3 186.7 %all-to-all-start = ((bf16[16,2,64,1536]{3,2,1,0:T(8,128)(2,1)}), bf16[16,2,64,1536]{3,2,1,0:T(8,128)(2,1)}, u32[]{:S(2)}, u32[]{:S(2)}) async-start(bf16[16,2,64,1536]{3,2,1,0:T(8,128)(2,1)} %copy.75), calls=%async_computation | async-start | bytes 12582912 | tf_op jit(solution)/shard_map/all_to_all | solution.py:77
  27.2 8.0 %copy-start.1 = (bf16[1,1,4,64,1536]{4,3,2,1,0:T(8,128)(2,1)S(1)}, bf16[1,1,4,64,1536]{4,3,2,1,0:T(8,128)(2,1)}, u32[]{:S(2)}) copy-start(bf16[1,1,4,64,1536]{4,3,2,1,0:T(8,128)(2,1)} %param.7) | copy-start | bytes 2359300
  27.2 167.6 %collective-permute-start = (bf16[2,4,64,1536]{3,1,2,0:T(4,128)(2,1)}, bf16[2,4,64,1536]{3,1,2,0:T(4,128)(2,1)}, u32[]{:S(2)}, u32[]{:S(2)}) collective-permute-start(bf16[2,4,64,1536]{3,1,2,0:T(4,128)(2,1)} %pad_maximum_fusion.1), channel_id=1, source_target_pairs={{0,2},{2,4},{4,6},{6,8},{8,10},{10,12},{12,14},{14,16},{16,18},{18... | collective-permute-start | bytes 4718600 | tf_op jit(solution)/shard_map/ppermute | solution.py:12
  218.9 2.5 copy-start.3
  359.8 0.9 copy-start.4
  377.0 1.7 copy-start
  395.0 185.4 %all-to-all-start.1 = ((bf16[16,2,64,1536]{3,2,1,0:T(8,128)(2,1)}), bf16[16,2,64,1536]{3,2,1,0:T(8,128)(2,1)}, u32[]{:S(2)}, u32[]{:S(2)}) async-start(bf16[16,2,64,1536]{3,2,1,0:T(8,128)(2,1)} %bitcast_multiply_fusion), calls=%async_computation.1 | async-start | bytes 12582912 | tf_op jit(solution)/shard_map/all_to_all | solution.py:144
  403.9 1.1 slice-start
  403.9 4.4 copy-start.2
  405.0 5.2 copy-start.5
  406.4 172.3 %collective-permute-start.1 = (bf16[2,256,1536]{1,2,0:T(8,128)(2,1)}, bf16[2,256,1536]{1,2,0:T(8,128)(2,1)}, u32[]{:S(2)}, u32[]{:S(2)}) collective-permute-start(bf16[2,256,1536]{1,2,0:T(8,128)(2,1)} %pad_maximum_fusion.2), channel_id=1, source_target_pairs={{2,0},{4,2},{6,4},{8,6},{10,8},{12,10},{14,12},{16,14},{18,16},{20... | collective-permute-start | bytes 4718600 | tf_op jit(solution)/shard_map/ppermute | solution.py:12
where the time goes:
time: 602 us; the launch traced here: 593 us
  waiting for transfers between devices  304 us (50%)
  matrix products  123 us (20%)
  local copies, waits for them, and re-layouts  96.4 us (16%)
  other arithmetic  41.1 us (7%)
  starting transfers between devices  25.7 us (4%)
    ppermute x2, waiting for transfers between devices, from_behind(): return lax.ppermute(value, axis, pairs)  304 us
    dot_general x12, matrix products, head_pass(): jnp.einsum('nm,ne->me', normalized_low, grad_rows, preferred_element_type...  24.7 us
    dot_general x12, matrix products, head_pass(): jnp.einsum('nm,me->ne', score_grad, key_rows, preferred_element_type=jnp....  22.5 us
    dot_general x12, matrix products, head_pass(): jnp.einsum('ne,me->nm', grad_rows, value_rows, preferred_element_type=jnp...  16.8 us
    dot_general x12, matrix products, head_pass(): jnp.einsum('nm,me->ne', normalized_low, value_rows, preferred_element_typ...  16.6 us
    dot_general x12, matrix products, head_pass(): jnp.einsum('ne,me->nm', query_rows, key_rows, preferred_element_type=jnp....  16.4 us
    dot_general x12, matrix products, head_pass(): jnp.einsum('nm,ne->me', score_grad, query_rows, preferred_element_type=jn...  14.3 us
    dynamic_update_slice x24, local copies, waits for them, and re-layouts, body(): lax.map(one_head, head_inputs)  12.4 us
  transfers between devices with their start and end apart: 4, of which 2 were waited for; matrix products, arithmetic and copies ran while one was open for 7% of the time, Pallas kernels for 0%

commit v1 on v0

v1 whole, which is shorter than its diff:
```python
import functools

import jax
import jax.numpy as jnp
from jax import lax
from jax.experimental import pallas as pl
from jax.experimental.pallas import tpu as pltpu
from jax.sharding import PartitionSpec as P

HEAD_DIM = 128
MESH = pl.DeviceIdType.MESH
F32 = jnp.float32
BF16 = jnp.bfloat16


def dot(a, b, over_a, over_b):
    return lax.dot_general(a, b, (((over_a,), (over_b,)), ((), ())), preferred_element_type=F32)


def kernel(
    views, frames, columns, tile_rows, heads,
    q_in, k_in, v_in, g_in, epi, holds, o_out, dq_out, dk_out, dv_out,
    q_buf, g_buf, kv_buf, line_buf, pick, terms, own, later, back, results,
    local_sem, pre_send, pre_recv, frame_send, frame_recv, line_send, line_recv,
    later_send, later_recv, back_send, back_recv, post_send, post_recv, out_sem,
):
    view = lax.axis_index("view")
    frame = lax.axis_index("tm")
    height = lax.axis_index("height")
    other = 1 - height
    tokens = tile_rows * columns
    others = views - 1
    set_size = 2 * tokens + others * columns
    scale = HEAD_DIM ** (-0.5)
    inputs = (q_in, k_in, v_in, g_in)
    outputs = (o_out, dq_out, dk_out, dv_out)
    partner = {"height": other}

    def requester(d):
        return lax.rem(view - d + views, views)

    def source(d):
        return lax.rem(view + d, views)

    def cols(group, j):
        return pl.ds(pl.multiple_of((group * heads + j) * HEAD_DIM, HEAD_DIM), HEAD_DIM)

    def landing(a, j, band):
        if a == 0:
            return q_buf.at[j, band]
        if a == 3:
            return g_buf.at[j, band]
        return kv_buf.at[j, a - 1, band, pl.ds(0, tokens)]

    def local_copy(a, j):
        return pltpu.make_async_copy(
            inputs[a].at[:, cols(height, j)], landing(a, j, height), local_sem.at[j, a]
        )

    def pre_copy(a, j):
        return pltpu.make_async_remote_copy(
            src_ref=inputs[a].at[:, cols(other, j)],
            dst_ref=landing(a, j, height),
            send_sem=pre_send.at[j, a],
            recv_sem=pre_recv.at[j, a],
            device_id=partner,
            device_id_type=MESH,
        )

    def pre_arrival(a, j):
        return pltpu.make_async_remote_copy(
            src_ref=inputs[a].at[:, cols(other, j)],
            dst_ref=landing(a, j, other),
            send_sem=pre_send.at[j, a],
            recv_sem=pre_recv.at[j, a],
            device_id=partner,
            device_id_type=MESH,
        )

    def frame_copy(j):
        return pltpu.make_async_remote_copy(
            src_ref=kv_buf.at[j, :, :, pl.ds(0, tokens)],
            dst_ref=kv_buf.at[j, :, :, pl.ds(tokens, tokens)],
            send_sem=frame_send.at[j],
            recv_sem=frame_recv.at[j],
            device_id={"tm": lax.rem(frame + 1, frames)},
            device_id_type=MESH,
        )

    def later_copy(j):
        return pltpu.make_async_remote_copy(
            src_ref=terms.at[j, :, :, pl.ds(0, tokens)],
            dst_ref=later.at[j],
            send_sem=later_send.at[j],
            recv_sem=later_recv.at[j],
            device_id={"tm": lax.rem(frame + frames - 1, frames)},
            device_id_type=MESH,
        )

    def line_copy(d, j):
        at = (d - 1) * columns
        return pltpu.make_async_remote_copy(
            src_ref=line_buf.at[j, :, :, pl.ds(at, columns)],
            dst_ref=kv_buf.at[j, :, :, pl.ds(2 * tokens + at, columns)],
            send_sem=line_send.at[j, d - 1],
            recv_sem=line_recv.at[j, d - 1],
            device_id={"view": requester(d)},
            device_id_type=MESH,
        )

    def back_copy(d, j):
        at = (d - 1) * columns
        return pltpu.make_async_remote_copy(
            src_ref=terms.at[j, :, :, pl.ds(tokens + at, columns)],
            dst_ref=back.at[j, :, :, pl.ds(at, columns)],
            send_sem=back_send.at[j, d - 1],
            recv_sem=back_recv.at[j, d - 1],
            device_id={"view": source(d)},
            device_id_type=MESH,
        )

    def out_copy(a, j):
        return pltpu.make_async_copy(
            results.at[a, j, height], outputs[a].at[:, cols(height, j)], out_sem.at[j, a]
        )

    def post_copy(a, j):
        return pltpu.make_async_remote_copy(
            src_ref=results.at[a, j, other],
            dst_ref=outputs[a].at[:, cols(height, j)],
            send_sem=post_send.at[j, a],
            recv_sem=post_recv.at[j, a],
            device_id=partner,
            device_id_type=MESH,
        )

    def post_arrival(a, j):
        return pltpu.make_async_remote_copy(
            src_ref=results.at[a, j, other],
            dst_ref=outputs[a].at[:, cols(other, j)],
            send_sem=post_send.at[j, a],
            recv_sem=post_recv.at[j, a],
            device_id=partner,
            device_id_type=MESH,
        )

    def start_local(j, carry):
        for a in range(4):
            local_copy(a, j).start()
        return carry

    lax.fori_loop(0, heads, start_local, 0)

    barrier = pltpu.get_barrier_semaphore()

    def greet(device):
        pl.semaphore_signal(barrier, inc=1, device_id=device, device_id_type=MESH)

    greet(partner)
    for d in range(1, views):
        greet({"view": source(d)})
    greet({"tm": lax.rem(frame + 1, frames)})
    greet({"tm": lax.rem(frame + frames - 1, frames)})
    pl.semaphore_wait(barrier, views + 2)

    def start_pre(j):
        for a in (1, 2, 0, 3):
            pre_copy(a, j).start()

    start_pre(0)
    start_pre(1)

    @pl.when(frame == 0)
    def _():
        kv_buf[:, :, :, tokens : 2 * tokens, :] = jnp.zeros(
            (heads, 2, 2, tokens, HEAD_DIM), BF16
        )

    @pl.when(frame == frames - 1)
    def _():
        later[...] = jnp.zeros(later.shape, BF16)

    def gather(j):
        for a in range(4):
            local_copy(a, j).wait()
            pre_arrival(a, j).wait_recv()

        @pl.when(frame < frames - 1)
        def _():
            frame_copy(j).start()

        for side in range(2):
            for band in range(2):
                for row in range(tile_rows):
                    pick[side, band * tile_rows + row] = kv_buf[
                        j, side, band, row * columns : (row + 1) * columns, :
                    ]
        for d in range(1, views):
            for band in range(2):
                row = epi[requester(d), 0, band, d - 1]
                for side in range(2):
                    line_buf[j, side, band, (d - 1) * columns : d * columns, :] = pick[side, row]
            line_copy(d, j).start()

        @pl.when(j < heads - 2)
        def _():
            for a in range(4):
                pre_copy(a, j).wait_send()
            start_pre(j + 2)

    first_row = lax.broadcasted_iota(jnp.int32, (set_size, 1), 0)
    masked = (first_row >= tokens) & (first_row < 2 * tokens) & (frame == 0)
    bias = jnp.where(masked, -1e30, 0.0).astype(F32)

    def attend(j, band):
        queries = q_buf[j, band]
        grads = g_buf[j, band]
        keys = kv_buf[j, 0, band]
        values = kv_buf[j, 1, band]
        scores = dot(keys, queries, 1, 1) * scale + bias
        weights = jnp.exp(scores - jnp.max(scores, axis=0, keepdims=True))
        probs = weights * (1.0 / jnp.sum(weights, axis=0, keepdims=True))
        probs_low = probs.astype(BF16)
        attended = dot(values, probs_low, 0, 0).astype(BF16)
        results[0, j, band] = attended.astype(F32).T.astype(BF16)
        delta = jnp.sum(
            grads.astype(F32).T * attended.astype(F32), axis=0, keepdims=True
        )
        dprobs = dot(values, grads, 1, 1)
        dscores = (probs * (dprobs - delta)).astype(BF16)
        dq = dot(keys, dscores, 0, 0) * scale
        results[1, j, band] = dq.T.astype(BF16)
        dk = dot(dscores, queries, 1, 0) * scale
        dv = dot(probs_low, grads, 1, 0)
        for side, term in ((0, dk), (1, dv)):
            own[j, side, band] = term[:tokens]
            terms[j, side, band] = term[tokens:].astype(BF16)

    def compute(j):
        @pl.when(frame > 0)
        def _():
            frame_copy(j).wait_recv()

        for d in range(1, views):
            line_copy(d, j).wait_recv()

        def one_band(band, carry):
            attend(j, band)
            return carry

        lax.fori_loop(0, 2, one_band, 0)

        @pl.when(frame > 0)
        def _():
            later_copy(j).start()

        for d in range(1, views):
            back_copy(d, j).start()
        for a in range(2):
            post_copy(a, j).start()
            out_copy(a, j).start()

    def settle(j):
        @pl.when(frame < frames - 1)
        def _():
            later_copy(j).wait_recv()

        for d in range(1, views):
            back_copy(d, j).wait_recv()

        step = 16
        chunks = columns // step

        def chunk(i, carry):
            side = i // chunks
            at = pl.multiple_of((i % chunks) * step, step)
            sums = []
            for row in range(2 * tile_rows):
                here = pl.ds((row % tile_rows) * columns + at, step)
                band = row // tile_rows
                sums.append(own[j, side, band, here, :] + later[j, side, band, here, :].astype(F32))
            for d in range(1, views):
                for band in range(2):
                    slot = back[j, side, band, pl.ds((d - 1) * columns + at, step), :].astype(F32)
                    for row in range(2 * tile_rows):
                        sums[row] += slot * holds[band, d - 1, row]
            for row in range(2 * tile_rows):
                here = pl.ds((row % tile_rows) * columns + at, step)
                results[2 + side, j, row // tile_rows, here, :] = sums[row].astype(BF16)
            return carry

        lax.fori_loop(0, 2 * chunks, chunk, 0)
        for a in range(2, 4):
            post_copy(a, j).start()
            out_copy(a, j).start()

    def stage(t, carry):
        @pl.when(t < heads)
        def _():
            gather(t)

        @pl.when((t >= 1) & (t < heads + 1))
        def _():
            compute(t - 1)

        @pl.when(t >= 2)
        def _():
            settle(t - 2)

        return carry

    lax.fori_loop(0, heads + 2, stage, 0)

    def drain(j, carry):
        @pl.when(j >= heads - 2)
        def _():
            for a in range(4):
                pre_copy(a, j).wait_send()

        @pl.when(frame < frames - 1)
        def _():
            frame_copy(j).wait_send()

        @pl.when(frame > 0)
        def _():
            later_copy(j).wait_send()

        for d in range(1, views):
            line_copy(d, j).wait_send()
            back_copy(d, j).wait_send()
        for a in range(4):
            post_copy(a, j).wait_send()
            post_arrival(a, j).wait_recv()
            out_copy(a, j).wait()
        return carry

    lax.fori_loop(0, heads, drain, 0)


def body(query_vectors, key_vectors, value_vectors, out_grad, epi_rows):
    views = lax.axis_size("view")
    frames = lax.axis_size("tm")
    bands = lax.axis_size("height")
    shape = query_vectors.shape
    tile_rows, columns, features = shape[2:]
    tokens = tile_rows * columns
    heads = features // HEAD_DIM // bands
    others = views - 1
    set_size = 2 * tokens + others * columns
    flat = [x.reshape(tokens, features) for x in (query_vectors, key_vectors, value_vectors, out_grad)]
    viewers = jnp.arange(views, dtype=jnp.int32)
    theirs = (lax.axis_index("view") - viewers) % views
    asked = theirs[:, None] == jnp.arange(1, views, dtype=jnp.int32)[None, :]
    rows = jnp.sum(epi_rows[:, 0] * asked[:, None, :], axis=0)
    holds = (rows[:, :, None] == jnp.arange(bands * tile_rows, dtype=jnp.int32)).astype(F32)
    dma = pltpu.SemaphoreType.DMA
    outs = pl.pallas_call(
        functools.partial(kernel, views, frames, columns, tile_rows, heads),
        out_shape=[jax.ShapeDtypeStruct((tokens, features), BF16)] * 4,
        in_specs=[pl.BlockSpec(memory_space=pl.ANY)] * 4 + [pl.BlockSpec(memory_space=pltpu.SMEM)] * 2,
        out_specs=[pl.BlockSpec(memory_space=pl.ANY)] * 4,
        scratch_shapes=[
            pltpu.VMEM((heads, 2, tokens, HEAD_DIM), BF16),
            pltpu.VMEM((heads, 2, tokens, HEAD_DIM), BF16),
            pltpu.VMEM((heads, 2, 2, set_size, HEAD_DIM), BF16),
            pltpu.VMEM((heads, 2, 2, others * columns, HEAD_DIM), BF16),
            pltpu.VMEM((2, 2 * tile_rows, columns, HEAD_DIM), BF16),
            pltpu.VMEM((heads, 2, 2, set_size - tokens, HEAD_DIM), BF16),
            pltpu.VMEM((heads, 2, 2, tokens, HEAD_DIM), F32),
            pltpu.VMEM((heads, 2, 2, tokens, HEAD_DIM), BF16),
            pltpu.VMEM((heads, 2, 2, others * columns, HEAD_DIM), BF16),
            pltpu.VMEM((4, heads, 2, tokens, HEAD_DIM), BF16),
            dma((heads, 4)),
            dma((heads, 4)),
            dma((heads, 4)),
            dma((heads,)),
            dma((heads,)),
            dma((heads, others)),
            dma((heads, others)),
            dma((heads,)),
            dma((heads,)),
            dma((heads, others)),
            dma((heads, others)),
            dma((heads, 4)),
            dma((heads, 4)),
            dma((heads, 4)),
        ],
        compiler_params=pltpu.CompilerParams(
            collective_id=0, has_side_effects=True, vmem_limit_bytes=52 * 1024 * 1024
        ),
        name="attention",
    )(*flat, epi_rows, holds)
    return tuple(x.reshape(shape) for x in outs)


def solution(mesh):
    tiled = P("view", "tm", "height", None, None)
    return jax.shard_map(
        body,
        mesh=mesh,
        in_specs=(tiled, tiled, tiled, tiled, P(None, "tm", None, None)),
        out_specs=(tiled, tiled, tiled, tiled),
        check_vma=False,
    )
```

time: 602 us -> 204 us (0.34)
  the two profiles are of different devices: /device:TPU:22 before, /device:TPU:38 now
where the time goes in v1:
time: 204 us; the launch traced here: 203 us
  Pallas kernels  197 us (97%)
  local copies, waits for them, and re-layouts  5.39 us (3%)
    pallas_call x1, Pallas kernels, body(): pl.pallas_call(functools.partial(kernel, views, frames, columns, tile_row...  197 us
    unnamed x11, local copies, waits for them, and re-layouts  5.29 us

profile of v1, /device:TPU:38, one launch (start us, length us, event | category | flops | bytes accessed | tf_op | source)
XLA Modules:
  0.0 203.3 jit_solution(9480696929196463386)
XLA Ops:
  0.6 0.0 copy-start.2
  0.7 0.1 compare_convert_fusion
  0.7 0.6 copy-done.2
  1.3 0.2 fusion.1
  1.6 0.1 copy.10
  1.7 0.1 fusion.holds
  1.7 0.1 copy.11.epi
  1.8 196.9 %attention.1 = (bf16[256,1536]{1,0:T(8,128)(2,1)S(1)}, bf16[256,1536]{1,0:T(8,128)(2,1)S(1)}, bf16[256,1536]{1,0:T(8,128)(2,1)}, bf16[256,1536]{1,0:T(8,128)(2,1)}) custom-call(bf16[256,1536]{1,0:T(8,128)(2,1)} %bitcast.16, bf16[256,1536]{1,0:T(8,128)(2,1)} %bitcast.17, bf16[256,1536]{1,0:T(8,128)(2,1)} %bitcast.18, bf16[256,1536]{1,0:T(8,128)(2,1)} %bitcast.19, ...), custom_call_target="tpu_custom_call" | custom-call | tf_op jit(solution)/shard_map/attention/pallas_call | solution.py:357
  198.7 0.9 copy.16
  199.6 0.0 copy-start.1
  199.6 0.9 copy.17
  200.5 0.5 copy-done.1
  201.0 0.0 copy-start
  201.0 0.9 copy.18
  201.9 0.5 copy-done
  202.4 0.9 copy.19
  (2 shorter events, 0.0 us)
Async XLA Ops:
  0.6 0.7 copy-start.2
  199.6 1.4 copy-start.1
  201.0 1.4 copy-start

commit v2 on v1

--- a/solution.py
+++ b/solution.py
@@ -8,6 +8,12 @@
 from jax.sharding import PartitionSpec as P
 
 HEAD_DIM = 128
+RUN = 4
+EARLY = 3
+LAG_AHEAD = 0
+LAG_COMPUTE = 2
+LAG_BEHIND = 2
+LAG_SETTLE = 3
 MESH = pl.DeviceIdType.MESH
 F32 = jnp.float32
 BF16 = jnp.bfloat16
@@ -20,9 +26,9 @@
 def kernel(
     views, frames, columns, tile_rows, heads,
     q_in, k_in, v_in, g_in, epi, holds, o_out, dq_out, dk_out, dv_out,
-    q_buf, g_buf, kv_buf, line_buf, pick, terms, own, later, back, results,
+    q_buf, g_buf, kv_buf, line_buf, pick, terms, own, later, back, results, ahead, behind,
     local_sem, pre_send, pre_recv, frame_send, frame_recv, line_send, line_recv,
-    later_send, later_recv, back_send, back_recv, post_send, post_recv, out_sem,
+    later_send, later_recv, ahead_send, ahead_recv, behind_send, behind_recv, back_send, back_recv, post_send, post_recv, out_sem,
 ):
     view = lax.axis_index("view")
     frame = lax.axis_index("tm")
@@ -77,25 +83,121 @@
             device_id_type=MESH,
         )
 
-    def frame_copy(j):
-        return pltpu.make_async_remote_copy(
-            src_ref=kv_buf.at[j, :, :, pl.ds(0, tokens)],
-            dst_ref=kv_buf.at[j, :, :, pl.ds(tokens, tokens)],
-            send_sem=frame_send.at[j],
-            recv_sem=frame_recv.at[j],
-            device_id={"tm": lax.rem(frame + 1, frames)},
-            device_id_type=MESH,
-        )
-
-    def later_copy(j):
-        return pltpu.make_async_remote_copy(
-            src_ref=terms.at[j, :, :, pl.ds(0, tokens)],
-            dst_ref=later.at[j],
-            send_sem=later_send.at[j],
-            recv_sem=later_recv.at[j],
-            device_id={"tm": lax.rem(frame + frames - 1, frames)},
-            device_id_type=MESH,
-        )
+    run_at = lax.rem(frame, RUN)
+    run_start = frame - run_at
+
+    def at_frame(f):
+        return {"tm": lax.rem(f + frames, frames)}
+
+    def remote(src, dst, send_sem, recv_sem, device):
+        return pltpu.make_async_remote_copy(
+            src_ref=src,
+            dst_ref=dst,
+            send_sem=send_sem,
+            recv_sem=recv_sem,
+            device_id=device,
+            device_id_type=MESH,
+        )
+
+    def earlier_slot(p, j):
+        return kv_buf.at[j, p // 2, p % 2, pl.ds(tokens, tokens)]
+
+    def frame_copy(p, j):
+        return remote(
+            kv_buf.at[j, p // 2, p % 2, pl.ds(0, tokens)],
+            earlier_slot(p, j),
+            frame_send.at[j, p],
+            frame_recv.at[j, p],
+            at_frame(frame + 1),
+        )
+
+    def ahead_copy(p, j):
+        return remote(
+            kv_buf.at[j, p // 2, p % 2, pl.ds(0, tokens)],
+            ahead.at[j],
+            frame_send.at[j, p],
+            ahead_recv.at[j],
+            at_frame(run_start + p),
+        )
+
+    def ahead_pass(j):
+        return remote(
+            ahead.at[j],
+            earlier_slot(run_at, j),
+            ahead_send.at[j],
+            frame_recv.at[j, run_at],
+            at_frame(run_start + RUN),
+        )
+
+    def later_copy(p, j):
+        return remote(
+            terms.at[j, p // 2, p % 2, pl.ds(0, tokens)],
+            later.at[j, p // 2, p % 2],
+            later_send.at[j, p],
+            later_recv.at[j, p],
+            at_frame(frame - 1),
+        )
+
+    def behind_copy(p, j):
+        return remote(
+            terms.at[j, p // 2, p % 2, pl.ds(0, tokens)],
+            behind.at[j],
+            later_send.at[j, p],
+            behind_recv.at[j],
+            at_frame(run_start + p),
+        )
+
+    def behind_pass(j):
+        return remote(
+            behind.at[j],
+            later.at[j, run_at // 2, run_at % 2],
+            behind_send.at[j],
+            later_recv.at[j, run_at],
+            at_frame(run_start - 1),
+        )
+
+    passes_ahead = (run_at < RUN - 1) & (frame < frames - RUN)
+    passes_behind = (run_at > 0) & (frame >= RUN)
+
+    def send_frame(j):
+        @pl.when(run_at < RUN - 1)
+        def _():
+            for p in range(RUN):
+                frame_copy(p, j).start()
+
+        @pl.when((run_at == RUN - 1) & (frame < frames - 1))
+        def _():
+            frame_copy(RUN - 1, j).start()
+            for p in range(RUN - 1):
+                ahead_copy(p, j).start()
+
+    def send_later(j):
+        @pl.when(run_at > 0)
+        def _():
+            for p in range(RUN):
+                later_copy(p, j).start()
+
+        @pl.when((run_at == 0) & (frame > 0))
+        def _():
+            later_copy(0, j).start()
+            for p in range(1, RUN):
+                behind_copy(p, j).start()
+
+    def pass_ahead(j):
+        @pl.when(passes_ahead)
+        def _():
+            remote(
+                ahead.at[j], ahead.at[j], ahead_send.at[j], ahead_recv.at[j], at_frame(run_start + RUN)
+            ).wait_recv()
+            ahead_pass(j).start()
+
+    def pass_behind(j):
+        @pl.when(passes_behind)
+        def _():
+            remote(
+                behind.at[j], behind.at[j], behind_send.at[j], behind_recv.at[j], at_frame(run_start - 1)
+            ).wait_recv()
+            behind_pass(j).start()
 
     def line_copy(d, j):
         at = (d - 1) * columns
@@ -159,16 +261,17 @@
     greet(partner)
     for d in range(1, views):
         greet({"view": source(d)})
-    greet({"tm": lax.rem(frame + 1, frames)})
-    greet({"tm": lax.rem(frame + frames - 1, frames)})
-    pl.semaphore_wait(barrier, views + 2)
+    for by in range(1, RUN + 1):
+        greet(at_frame(frame + by))
+        greet(at_frame(frame - by))
+    pl.semaphore_wait(barrier, views + 2 * RUN)
 
     def start_pre(j):
         for a in (1, 2, 0, 3):
             pre_copy(a, j).start()
 
-    start_pre(0)
-    start_pre(1)
+    for j in range(min(EARLY, heads)):
+        start_pre(j)
 
     @pl.when(frame == 0)
     def _():
@@ -185,9 +288,7 @@
             local_copy(a, j).wait()
             pre_arrival(a, j).wait_recv()
 
-        @pl.when(frame < frames - 1)
-        def _():
-            frame_copy(j).start()
+        send_frame(j)
 
         for side in range(2):
             for band in range(2):
@@ -202,11 +303,11 @@
                     line_buf[j, side, band, (d - 1) * columns : d * columns, :] = pick[side, row]
             line_copy(d, j).start()
 
-        @pl.when(j < heads - 2)
+        @pl.when(j < heads - EARLY)
         def _():
             for a in range(4):
                 pre_copy(a, j).wait_send()
-            start_pre(j + 2)
+            start_pre(j + EARLY)
 
     first_row = lax.broadcasted_iota(jnp.int32, (set_size, 1), 0)
     masked = (first_row >= tokens) & (first_row < 2 * tokens) & (frame == 0)
@@ -239,7 +340,8 @@
     def compute(j):
         @pl.when(frame > 0)
         def _():
-            frame_copy(j).wait_recv()
+            for p in range(RUN):
+                frame_copy(p, j).wait_recv()
 
         for d in range(1, views):
             line_copy(d, j).wait_recv()
@@ -250,9 +352,7 @@
 
         lax.fori_loop(0, 2, one_band, 0)
 
-        @pl.when(frame > 0)
-        def _():
-            later_copy(j).start()
+        send_later(j)
 
         for d in range(1, views):
             back_copy(d, j).start()
@@ -263,7 +363,8 @@
     def settle(j):
         @pl.when(frame < frames - 1)
         def _():
-            later_copy(j).wait_recv()
+            for p in range(RUN):
+                later_copy(p, j).wait_recv()
 
         for d in range(1, views):
             back_copy(d, j).wait_recv()
@@ -295,35 +396,43 @@
             out_copy(a, j).start()
 
     def stage(t, carry):
-        @pl.when(t < heads)
-        def _():
-            gather(t)
-
-        @pl.when((t >= 1) & (t < heads + 1))
-        def _():
-            compute(t - 1)
-
-        @pl.when(t >= 2)
-        def _():
-            settle(t - 2)
-
+        def at_stage(lag, step):
+            @pl.when((t >= lag) & (t < heads + lag))
+            def _():
+                step(t - lag)
+
+        at_stage(0, gather)
+        at_stage(LAG_COMPUTE, compute)
+        at_stage(LAG_AHEAD, pass_ahead)
+        at_stage(LAG_SETTLE, settle)
+        at_stage(LAG_BEHIND, pass_behind)
         return carry
 
-    lax.fori_loop(0, heads + 2, stage, 0)
+    lax.fori_loop(0, heads + LAG_SETTLE, stage, 0)
 
     def drain(j, carry):
-        @pl.when(j >= heads - 2)
+        @pl.when(j >= heads - EARLY)
         def _():
             for a in range(4):
                 pre_copy(a, j).wait_send()
 
         @pl.when(frame < frames - 1)
         def _():
-            frame_copy(j).wait_send()
+            for p in range(RUN):
+                frame_copy(p, j).wait_send()
 
         @pl.when(frame > 0)
         def _():
-            later_copy(j).wait_send()
+            for p in range(RUN):
+                later_copy(p, j).wait_send()
+
+        @pl.when(passes_ahead)
+        def _():
+            ahead_pass(j).wait_send()
+
+        @pl.when(passes_behind)
+        def _():
+            behind_pass(j).wait_send()
 
         for d in range(1, views):
             line_copy(d, j).wait_send()
@@ -370,13 +479,19 @@
             pltpu.VMEM((heads, 2, 2, tokens, HEAD_DIM), BF16),
             pltpu.VMEM((heads, 2, 2, others * columns, HEAD_DIM), BF16),
             pltpu.VMEM((4, heads, 2, tokens, HEAD_DIM), BF16),
+            pltpu.VMEM((heads, tokens, HEAD_DIM), BF16),
+            pltpu.VMEM((heads, tokens, HEAD_DIM), BF16),
             dma((heads, 4)),
             dma((heads, 4)),
             dma((heads, 4)),
+            dma((heads, RUN)),
+            dma((heads, RUN)),
+            dma((heads, others)),
+            dma((heads, others)),
+            dma((heads, RUN)),
+            dma((heads, RUN)),
             dma((heads,)),
             dma((heads,)),
-            dma((heads, others)),
-            dma((heads, others)),
             dma((heads,)),
             dma((heads,)),
             dma((heads, others)),

time: 204 us -> 172 us (0.84)
  the two profiles are of different devices: /device:TPU:38 before, /device:TPU:22 now
where the time goes in v2:
time: 172 us; the launch traced here: 169 us
  Pallas kernels  162 us (94%)
  local copies, waits for them, and re-layouts  5.39 us (3%)
    pallas_call x1, Pallas kernels, body(): pl.pallas_call(functools.partial(kernel, views, frames, columns, tile_row...  162 us
    unnamed x11, local copies, waits for them, and re-layouts  5.29 us

profile of v2, /device:TPU:22, one launch (start us, length us, event | category | flops | bytes accessed | tf_op | source)
XLA Modules:
  0.0 168.9 jit_solution(5270229401654597038)
XLA Ops:
  0.6 0.0 copy-start.2
  0.7 0.1 compare_convert_fusion
  0.7 0.6 copy-done.2
  1.3 0.2 fusion.1
  1.6 0.1 copy.10
  1.7 0.1 fusion.holds
  1.7 0.1 copy.11.epi
  1.8 162.4 %attention.1 = (bf16[256,1536]{1,0:T(8,128)(2,1)S(1)}, bf16[256,1536]{1,0:T(8,128)(2,1)S(1)}, bf16[256,1536]{1,0:T(8,128)(2,1)}, bf16[256,1536]{1,0:T(8,128)(2,1)}) custom-call(bf16[256,1536]{1,0:T(8,128)(2,1)} %bitcast.16, bf16[256,1536]{1,0:T(8,128)(2,1)} %bitcast.17, bf16[256,1536]{1,0:T(8,128)(2,1)} %bitcast.18, bf16[256,1536]{1,0:T(8,128)(2,1)} %bitcast.19, ...), custom_call_target="tpu_custom_call" | custom-call | tf_op jit(solution)/shard_map/attention/pallas_call | solution.py:466
  164.3 0.9 copy.16
  165.2 0.0 copy-start.1
  165.2 0.9 copy.17
  166.0 0.5 copy-done.1
  166.6 0.0 copy-start
  166.6 0.9 copy.18
  167.5 0.5 copy-done
  168.0 0.9 copy.19
  (2 shorter events, 0.0 us)
Async XLA Ops:
  0.6 0.7 copy-start.2
  165.2 1.4 copy-start.1
  166.6 1.4 copy-start

commit v3 on v2

--- a/solution.py
+++ b/solution.py
@@ -9,11 +9,13 @@
 
 HEAD_DIM = 128
 RUN = 4
+RELAYED = 5
 EARLY = 3
+QUERIES_BEHIND = 2
 LAG_AHEAD = 0
-LAG_COMPUTE = 2
-LAG_BEHIND = 2
-LAG_SETTLE = 3
+LAG_COMPUTE = 3
+LAG_BEHIND = 3
+LAG_SETTLE = 4
 MESH = pl.DeviceIdType.MESH
 F32 = jnp.float32
 BF16 = jnp.bfloat16
@@ -177,11 +179,16 @@
             for p in range(RUN):
                 later_copy(p, j).start()
 
-        @pl.when((run_at == 0) & (frame > 0))
+        @pl.when((run_at == 0) & (frame > 0) & (j < RELAYED))
         def _():
             later_copy(0, j).start()
             for p in range(1, RUN):
                 behind_copy(p, j).start()
+
+        @pl.when((run_at == 0) & (frame > 0) & (j >= RELAYED))
+        def _():
+            for p in range(RUN):
+                later_copy(p, j).start()
 
     def pass_ahead(j):
         @pl.when(passes_ahead)
@@ -192,7 +199,7 @@
             ahead_pass(j).start()
 
     def pass_behind(j):
-        @pl.when(passes_behind)
+        @pl.when(passes_behind & (j < RELAYED))
         def _():
             remote(
                 behind.at[j], behind.at[j], behind_send.at[j], behind_recv.at[j], at_frame(run_start - 1)
@@ -266,12 +273,18 @@
         greet(at_frame(frame - by))
     pl.semaphore_wait(barrier, views + 2 * RUN)
 
-    def start_pre(j):
-        for a in (1, 2, 0, 3):
-            pre_copy(a, j).start()
+    def start_pair(j):
+        pre_copy(1, j).start()
+        pre_copy(2, j).start()
+
+    def start_queries(j):
+        pre_copy(0, j).start()
+        pre_copy(3, j).start()
 
     for j in range(min(EARLY, heads)):
-        start_pre(j)
+        start_pair(j)
+    for j in range(min(EARLY - QUERIES_BEHIND, heads)):
+        start_queries(j)
 
     @pl.when(frame == 0)
     def _():
@@ -284,7 +297,7 @@
         later[...] = jnp.zeros(later.shape, BF16)
 
     def gather(j):
-        for a in range(4):
+        for a in (1, 2):
             local_copy(a, j).wait()
             pre_arrival(a, j).wait_recv()
 
@@ -305,9 +318,11 @@
 
         @pl.when(j < heads - EARLY)
         def _():
-            for a in range(4):
-                pre_copy(a, j).wait_send()
-            start_pre(j + EARLY)
+            start_pair(j + EARLY)
+
+        @pl.when(j < heads - EARLY + QUERIES_BEHIND)
+        def _():
+            start_queries(j + EARLY - QUERIES_BEHIND)
 
     first_row = lax.broadcasted_iota(jnp.int32, (set_size, 1), 0)
     masked = (first_row >= tokens) & (first_row < 2 * tokens) & (frame == 0)
@@ -338,6 +353,10 @@
             terms[j, side, band] = term[tokens:].astype(BF16)
 
     def compute(j):
+        for a in (0, 3):
+            local_copy(a, j).wait()
+            pre_arrival(a, j).wait_recv()
+
         @pl.when(frame > 0)
         def _():
             for p in range(RUN):
@@ -411,10 +430,8 @@
     lax.fori_loop(0, heads + LAG_SETTLE, stage, 0)
 
     def drain(j, carry):
-        @pl.when(j >= heads - EARLY)
-        def _():
-            for a in range(4):
-                pre_copy(a, j).wait_send()
+        for a in range(4):
+            pre_copy(a, j).wait_send()
 
         @pl.when(frame < frames - 1)
         def _():
@@ -430,7 +447,7 @@
         def _():
             ahead_pass(j).wait_send()
 
-        @pl.when(passes_behind)
+        @pl.when(passes_behind & (j < RELAYED))
         def _():
             behind_pass(j).wait_send()
 

time: 172 us -> 169 us (0.983); the launches traced: 169 us -> 168 us
  no operation moved by 1% of the time
where the time goes in v3:
time: 169 us; the launch traced here: 168 us
  Pallas kernels  162 us (96%)
  local copies, waits for them, and re-layouts  5.39 us (3%)
    pallas_call x1, Pallas kernels, body(): pl.pallas_call(functools.partial(kernel, views, frames, columns, tile_row...  162 us
    unnamed x11, local copies, waits for them, and re-layouts  5.29 us

profile of v3, /device:TPU:22, one launch (start us, length us, event | category | flops | bytes accessed | tf_op | source)
XLA Modules:
  0.0 168.3 jit_solution(1617375893301647779)
XLA Ops:
  0.6 0.0 copy-start.2
  0.7 0.1 compare_convert_fusion
  0.7 0.6 copy-done.2
  1.3 0.2 fusion.1
  1.6 0.1 copy.10
  1.7 0.1 fusion.holds
  1.7 0.1 copy.11.epi
  1.8 161.9 %attention.1 = (bf16[256,1536]{1,0:T(8,128)(2,1)S(1)}, bf16[256,1536]{1,0:T(8,128)(2,1)S(1)}, bf16[256,1536]{1,0:T(8,128)(2,1)}, bf16[256,1536]{1,0:T(8,128)(2,1)}) custom-call(bf16[256,1536]{1,0:T(8,128)(2,1)} %bitcast.16, bf16[256,1536]{1,0:T(8,128)(2,1)} %bitcast.17, bf16[256,1536]{1,0:T(8,128)(2,1)} %bitcast.18, bf16[256,1536]{1,0:T(8,128)(2,1)} %bitcast.19, ...), custom_call_target="tpu_custom_call" | custom-call | tf_op jit(solution)/shard_map/attention/pallas_call | solution.py:483
  163.7 0.9 copy.16
  164.6 0.0 copy-start.1
  164.6 0.9 copy.17
  165.5 0.5 copy-done.1
  166.0 0.0 copy-start
  166.0 0.9 copy.18
  166.9 0.5 copy-done
  167.5 0.9 copy.19
  (2 shorter events, 0.0 us)
Async XLA Ops:
  0.6 0.7 copy-start.2
  164.6 1.4 copy-start.1
  166.0 1.4 copy-start

commit v4 on v3

--- a/solution.py
+++ b/solution.py
@@ -27,8 +27,8 @@
 
 def kernel(
     views, frames, columns, tile_rows, heads,
-    q_in, k_in, v_in, g_in, epi, holds, o_out, dq_out, dk_out, dv_out,
-    q_buf, g_buf, kv_buf, line_buf, pick, terms, own, later, back, results, ahead, behind,
+    q_in, k_in, v_in, g_in, epi_in, o_out, dq_out, dk_out, dv_out,
+    q_buf, g_buf, kv_buf, line_buf, pick, terms, own, later, back, results, ahead, behind, epi, epi_sem,
     local_sem, pre_send, pre_recv, frame_send, frame_recv, line_send, line_recv,
     later_send, later_recv, ahead_send, ahead_recv, behind_send, behind_recv, back_send, back_recv, post_send, post_recv, out_sem,
 ):
@@ -259,6 +259,8 @@
         return carry
 
     lax.fori_loop(0, heads, start_local, 0)
+    rows_copy = pltpu.make_async_copy(epi_in, epi, epi_sem)
+    rows_copy.start()
 
     barrier = pltpu.get_barrier_semaphore()
 
@@ -285,6 +287,8 @@
         start_pair(j)
     for j in range(min(EARLY - QUERIES_BEHIND, heads)):
         start_queries(j)
+
+    rows_copy.wait()
 
     @pl.when(frame == 0)
     def _():
@@ -311,7 +315,7 @@
                     ]
         for d in range(1, views):
             for band in range(2):
-                row = epi[requester(d), 0, band, d - 1]
+                row = epi[0, d - 1, band, requester(d)]
                 for side in range(2):
                     line_buf[j, side, band, (d - 1) * columns : d * columns, :] = pick[side, row]
             line_copy(d, j).start()
@@ -401,9 +405,10 @@
                 sums.append(own[j, side, band, here, :] + later[j, side, band, here, :].astype(F32))
             for d in range(1, views):
                 for band in range(2):
+                    row_there = epi[0, d - 1, band, requester(d)]
                     slot = back[j, side, band, pl.ds((d - 1) * columns + at, step), :].astype(F32)
                     for row in range(2 * tile_rows):
-                        sums[row] += slot * holds[band, d - 1, row]
+                        sums[row] += slot * (row_there == row).astype(F32)
             for row in range(2 * tile_rows):
                 here = pl.ds((row % tile_rows) * columns + at, step)
                 results[2 + side, j, row // tile_rows, here, :] = sums[row].astype(BF16)
@@ -461,6 +466,21 @@
         return carry
 
     lax.fori_loop(0, heads, drain, 0)
+
+
+def place(a, b, c, d, a_out, b_out, c_out, d_out, sem):
+    part = a.shape[0] // 4
+    copies = [
+        pltpu.make_async_copy(
+            x.at[pl.ds(n * part, part)], y.at[pl.ds(n * part, part)], sem.at[i, n]
+        )
+        for i, (x, y) in enumerate(((a, a_out), (b, b_out), (c, c_out), (d, d_out)))
+        for n in range(4)
+    ]
+    for copy in copies:
+        copy.start()
+    for copy in copies:
+        copy.wait()
 
 
 def body(query_vectors, key_vectors, value_vectors, out_grad, epi_rows):
@@ -474,16 +494,11 @@
     others = views - 1
     set_size = 2 * tokens + others * columns
     flat = [x.reshape(tokens, features) for x in (query_vectors, key_vectors, value_vectors, out_grad)]
-    viewers = jnp.arange(views, dtype=jnp.int32)
-    theirs = (lax.axis_index("view") - viewers) % views
-    asked = theirs[:, None] == jnp.arange(1, views, dtype=jnp.int32)[None, :]
-    rows = jnp.sum(epi_rows[:, 0] * asked[:, None, :], axis=0)
-    holds = (rows[:, :, None] == jnp.arange(bands * tile_rows, dtype=jnp.int32)).astype(F32)
     dma = pltpu.SemaphoreType.DMA
     outs = pl.pallas_call(
         functools.partial(kernel, views, frames, columns, tile_rows, heads),
         out_shape=[jax.ShapeDtypeStruct((tokens, features), BF16)] * 4,
-        in_specs=[pl.BlockSpec(memory_space=pl.ANY)] * 4 + [pl.BlockSpec(memory_space=pltpu.SMEM)] * 2,
+        in_specs=[pl.BlockSpec(memory_space=pltpu.HBM)] * 5,
         out_specs=[pl.BlockSpec(memory_space=pl.ANY)] * 4,
         scratch_shapes=[
             pltpu.VMEM((heads, 2, tokens, HEAD_DIM), BF16),
@@ -498,6 +513,8 @@
             pltpu.VMEM((4, heads, 2, tokens, HEAD_DIM), BF16),
             pltpu.VMEM((heads, tokens, HEAD_DIM), BF16),
             pltpu.VMEM((heads, tokens, HEAD_DIM), BF16),
+            pltpu.SMEM((1, others, bands, views), jnp.int32),
+            dma,
             dma((heads, 4)),
             dma((heads, 4)),
             dma((heads, 4)),
@@ -518,10 +535,19 @@
             dma((heads, 4)),
         ],
         compiler_params=pltpu.CompilerParams(
-            collective_id=0, has_side_effects=True, vmem_limit_bytes=52 * 1024 * 1024
+            collective_id=0, has_side_effects=True, vmem_limit_bytes=101 * 512 * 1024
         ),
         name="attention",
-    )(*flat, epi_rows, holds)
+    )(*flat, jnp.transpose(epi_rows, (1, 3, 2, 0)))
+    outs = pl.pallas_call(
+        place,
+        out_shape=[jax.ShapeDtypeStruct((tokens, features), BF16)] * 4,
+        in_specs=[pl.BlockSpec(memory_space=pltpu.VMEM)] * 4,
+        out_specs=[pl.BlockSpec(memory_space=pltpu.HBM)] * 4,
+        scratch_shapes=[dma((4, 4))],
+        compiler_params=pltpu.CompilerParams(vmem_limit_bytes=8 * 1024 * 1024),
+        name="place",
+    )(*outs)
     return tuple(x.reshape(shape) for x in outs)
 
 

time: 169 us -> 165 us (0.976)
  local copies, waits for them, and re-layouts: 5.39 us -> 0.69 us
  Pallas kernels: 162 us -> 164 us
    unnamed x11 -> x2, local copies, waits for them, and re-layouts: 5.29 us -> 0.69 us
    pallas_call x0 -> x1, Pallas kernels: none -> 1.79 us  [body(): pl.pallas_call(place, out_shape=[jax.ShapeDtypeStruct((tokens, features),...]
where the time goes in v4:
time: 165 us
  Pallas kernels  164 us (99%)
    pallas_call x1, Pallas kernels, body(): pl.pallas_call(functools.partial(kernel, views, frames, columns, tile_row...  162 us

profile of v4, /device:TPU:22, one launch (start us, length us, event | category | flops | bytes accessed | tf_op | source)
XLA Modules:
  0.0 165.0 jit_solution(9898630516034907666)
XLA Ops:
  0.6 0.0 copy-start
  0.6 0.7 copy-done
  1.3 161.9 %attention.1 = (bf16[256,1536]{1,0:T(8,128)(2,1)S(1)}, bf16[256,1536]{1,0:T(8,128)(2,1)S(1)}, bf16[256,1536]{1,0:T(8,128)(2,1)S(1)}, bf16[256,1536]{1,0:T(8,128)(2,1)S(1)}) custom-call(bf16[256,1536]{1,0:T(8,128)(2,1)} %bitcast.10, bf16[256,1536]{1,0:T(8,128)(2,1)} %bitcast.11, bf16[256,1536]{1,0:T(8,128)(2,1)} %bitcast.12, bf16[256,1536]{1,0:T(8,128)(2,1)} %bitcast.13, ...), custom_call_target="tpu_custom_call" | custom-call | tf_op jit(solution)/shard_map/attention/pallas_call | solution.py:498
  163.2 1.8 %place.1 = (bf16[256,1536]{1,0:T(8,128)(2,1)}, bf16[256,1536]{1,0:T(8,128)(2,1)}, bf16[256,1536]{1,0:T(8,128)(2,1)}, bf16[256,1536]{1,0:T(8,128)(2,1)}) custom-call(bf16[256,1536]{1,0:T(8,128)(2,1)S(1)} %get-tuple-element.12.a, bf16[256,1536]{1,0:T(8,128)(2,1)S(1)} %get-tuple-element.13.b, bf16[256,1536]{1,0:T(8,128)(2,1)S(1)} %get-tuple-element.14.c, ...), custom_call_target="tpu_custom_call" | custom-call | tf_op jit(solution)/shard_map/place/pallas_call | solution.py:542
Async XLA Ops:
  0.6 0.7 copy-start

commit v5 on v4

--- a/solution.py
+++ b/solution.py
@@ -253,15 +253,6 @@
             device_id_type=MESH,
         )
 
-    def start_local(j, carry):
-        for a in range(4):
-            local_copy(a, j).start()
-        return carry
-
-    lax.fori_loop(0, heads, start_local, 0)
-    rows_copy = pltpu.make_async_copy(epi_in, epi, epi_sem)
-    rows_copy.start()
-
     barrier = pltpu.get_barrier_semaphore()
 
     def greet(device):
@@ -273,6 +264,16 @@
     for by in range(1, RUN + 1):
         greet(at_frame(frame + by))
         greet(at_frame(frame - by))
+
+    def start_local(j, carry):
+        for a in range(4):
+            local_copy(a, j).start()
+        return carry
+
+    lax.fori_loop(0, heads, start_local, 0)
+    rows_copy = pltpu.make_async_copy(epi_in, epi, epi_sem)
+    rows_copy.start()
+
     pl.semaphore_wait(barrier, views + 2 * RUN)
 
     def start_pair(j):

time: 165 us -> 165 us (level)
  Pallas kernels: 164 us -> 162 us
where the time goes in v5:
time: 165 us; the launch traced here: 164 us
  Pallas kernels  162 us (98%)
    pallas_call x1, Pallas kernels, body(): pl.pallas_call(functools.partial(kernel, views, frames, columns, tile_row...  161 us

profile of v5, /device:TPU:22, one launch (start us, length us, event | category | flops | bytes accessed | tf_op | source)
XLA Modules:
  0.0 163.7 jit_solution(4934116947734988327)
XLA Ops:
  0.6 0.0 copy-start
  0.6 0.7 copy-done
  1.3 160.6 %attention.1 = (bf16[256,1536]{1,0:T(8,128)(2,1)S(1)}, bf16[256,1536]{1,0:T(8,128)(2,1)S(1)}, bf16[256,1536]{1,0:T(8,128)(2,1)S(1)}, bf16[256,1536]{1,0:T(8,128)(2,1)S(1)}) custom-call(bf16[256,1536]{1,0:T(8,128)(2,1)} %bitcast.10, bf16[256,1536]{1,0:T(8,128)(2,1)} %bitcast.11, bf16[256,1536]{1,0:T(8,128)(2,1)} %bitcast.12, bf16[256,1536]{1,0:T(8,128)(2,1)} %bitcast.13, ...), custom_call_target="tpu_custom_call" | custom-call | tf_op jit(solution)/shard_map/attention/pallas_call | solution.py:499
  162.0 1.8 %place.1 = (bf16[256,1536]{1,0:T(8,128)(2,1)}, bf16[256,1536]{1,0:T(8,128)(2,1)}, bf16[256,1536]{1,0:T(8,128)(2,1)}, bf16[256,1536]{1,0:T(8,128)(2,1)}) custom-call(bf16[256,1536]{1,0:T(8,128)(2,1)S(1)} %get-tuple-element.12.a, bf16[256,1536]{1,0:T(8,128)(2,1)S(1)} %get-tuple-element.13.b, bf16[256,1536]{1,0:T(8,128)(2,1)S(1)} %get-tuple-element.14.c, ...), custom_call_target="tpu_custom_call" | custom-call | tf_op jit(solution)/shard_map/place/pallas_call | solution.py:543
Async XLA Ops:
  0.6 0.7 copy-start

commit v6 on v5

--- a/solution.py
+++ b/solution.py
@@ -265,6 +265,21 @@
         greet(at_frame(frame + by))
         greet(at_frame(frame - by))
 
+    pl.semaphore_wait(barrier, views + 2 * RUN)
+
+    def start_pair(j):
+        pre_copy(1, j).start()
+        pre_copy(2, j).start()
+
+    def start_queries(j):
+        pre_copy(0, j).start()
+        pre_copy(3, j).start()
+
+    for j in range(min(EARLY, heads)):
+        start_pair(j)
+    for j in range(min(EARLY - QUERIES_BEHIND, heads)):
+        start_queries(j)
+
     def start_local(j, carry):
         for a in range(4):
             local_copy(a, j).start()
@@ -273,21 +288,6 @@
     lax.fori_loop(0, heads, start_local, 0)
     rows_copy = pltpu.make_async_copy(epi_in, epi, epi_sem)
     rows_copy.start()
-
-    pl.semaphore_wait(barrier, views + 2 * RUN)
-
-    def start_pair(j):
-        pre_copy(1, j).start()
-        pre_copy(2, j).start()
-
-    def start_queries(j):
-        pre_copy(0, j).start()
-        pre_copy(3, j).start()
-
-    for j in range(min(EARLY, heads)):
-        start_pair(j)
-    for j in range(min(EARLY - QUERIES_BEHIND, heads)):
-        start_queries(j)
 
     rows_copy.wait()
 

time: 165 us -> 165 us (level)
  no operation moved by 1% of the time
where the time goes in v6:
time: 165 us; the launch traced here: 164 us
  Pallas kernels  162 us (98%)
    pallas_call x1, Pallas kernels, body(): pl.pallas_call(functools.partial(kernel, views, frames, columns, tile_row...  161 us

profile of v6, /device:TPU:22, one launch (start us, length us, event | category | flops | bytes accessed | tf_op | source)
XLA Modules:
  0.0 163.7 jit_solution(2332782019394581825)
XLA Ops:
  0.6 0.0 copy-start
  0.6 0.7 copy-done
  1.3 160.6 %attention.1 = (bf16[256,1536]{1,0:T(8,128)(2,1)S(1)}, bf16[256,1536]{1,0:T(8,128)(2,1)S(1)}, bf16[256,1536]{1,0:T(8,128)(2,1)S(1)}, bf16[256,1536]{1,0:T(8,128)(2,1)S(1)}) custom-call(bf16[256,1536]{1,0:T(8,128)(2,1)} %bitcast.10, bf16[256,1536]{1,0:T(8,128)(2,1)} %bitcast.11, bf16[256,1536]{1,0:T(8,128)(2,1)} %bitcast.12, bf16[256,1536]{1,0:T(8,128)(2,1)} %bitcast.13, ...), custom_call_target="tpu_custom_call" | custom-call | tf_op jit(solution)/shard_map/attention/pallas_call | solution.py:499
  162.0 1.8 %place.1 = (bf16[256,1536]{1,0:T(8,128)(2,1)}, bf16[256,1536]{1,0:T(8,128)(2,1)}, bf16[256,1536]{1,0:T(8,128)(2,1)}, bf16[256,1536]{1,0:T(8,128)(2,1)}) custom-call(bf16[256,1536]{1,0:T(8,128)(2,1)S(1)} %get-tuple-element.12.a, bf16[256,1536]{1,0:T(8,128)(2,1)S(1)} %get-tuple-element.13.b, bf16[256,1536]{1,0:T(8,128)(2,1)S(1)} %get-tuple-element.14.c, ...), custom_call_target="tpu_custom_call" | custom-call | tf_op jit(solution)/shard_map/place/pallas_call | solution.py:543
Async XLA Ops:
  0.6 0.7 copy-start
